TPU v7x, 256 devices: a whole 4x4x8 slice. The times are simulated.
256 devices in a mesh: pb: 16 (over y_hi, z), ka: 16 (over x, y_lo, core).
Axes of the slice: x: 4, y: 4 (y_hi: 2, y_lo: 2; y = y_hi * 2 + y_lo), z: 8, core: 2. Of those that a mesh axis runs over, the one named last changes fastest.
Arguments:
- tokens: bfloat16 [16, 2048, 768], P('ka', 'pb'), may hold values from -6 to 6
- pair: bfloat16 [2048, 2048, 128], P('pb', 'ka'), may hold values from -500 to 500
- token_chain_index: int32 [2048], replicated, may hold values from 0 to 7, never falling along the last dimension, each value on 1 to 1024 neighbouring positions
- key_mask: int32 [2048], replicated, may hold values 0 or 1
- norm_gain: float32 [768], replicated, may hold values from 0.25 to 1.75
- pair_gain: float32 [128], replicated, may hold values from 0.1 to 1.9
- pair_proj: float32 [128, 16], replicated, may hold values from -0.140625 to 0.140625
- chain_gain: float32 [16], replicated, may hold values from -2 to 260
- w_qkvg: bfloat16 [768, 3072], replicated, may hold values from -0.21875 to 0.21875
- w_out: bfloat16 [768, 768], replicated, may hold values from -1.75 to 1.75
Outputs:
- update: bfloat16 [16, 2048, 768], P('ka', 'pb')
Inputs may be any that keep to these rules, and one draw needn't show every extreme that they name: `token_chain_index`: chain ids never fall along the tokens.
All inputs are finite; a program needn't handle non-finite values.
Results may differ from a plain program's by a relative error of at most 0.02.
Values may be sent and summed in bfloat16 or wider, within the bound.
No kernel may reach another device: no remote copies, remote signals or barrier semaphores. Data moves between devices by JAX's collectives and lax.ppermute only.
A program may use at most 128 MiB of HBM per device.

v0:
```python
import jax
import jax.numpy as jnp
from jax import lax
from jax.sharding import PartitionSpec as P

epsilon = 1e-05


def norm_rows(values, gain):
    values = values.astype(jnp.float32)
    center = jnp.mean(values, axis=-1, keepdims=True)
    spread = jnp.mean(jnp.square(values - center), axis=-1, keepdims=True)
    return (values - center) * lax.rsqrt(spread + epsilon) * gain


def pair_bias(pair_rows, pair_gain, pair_proj, chain_query, chain_keys, chain_gain):
    zhat = norm_rows(pair_rows, pair_gain)
    head_bias = jnp.einsum("qkc,ch->hqk", zhat, pair_proj, precision=lax.Precision.HIGHEST)
    same = (chain_query[:, None] == chain_keys[None, :]).astype(jnp.float32)
    return head_bias + chain_gain[:, None, None] * same[None]


def apply_attention(query_vectors, keys, values, bias, key_mask, heads):
    q_count = query_vectors.shape[0]
    k_count = keys.shape[0]
    width = query_vectors.shape[1]
    hdim = width // heads
    query_heads = query_vectors.reshape(q_count, heads, hdim)
    key_heads = keys.reshape(k_count, heads, hdim)
    value_heads = values.reshape(k_count, heads, hdim)
    scores = jnp.einsum("qhd,khd->hqk", query_heads, key_heads, preferred_element_type=jnp.float32)
    scores = scores * hdim ** (-0.5) + bias
    scores = jnp.where(key_mask[None, None, :] > 0, scores, jnp.float32(-1000000000.0))
    top = jnp.max(scores, axis=-1, keepdims=True)
    expo = jnp.exp(scores - top)
    total = jnp.sum(expo, axis=-1)
    summed = jnp.einsum(
        "hqk,khd->qhd", expo.astype(jnp.bfloat16), value_heads, preferred_element_type=jnp.float32
    )
    return (summed / jnp.transpose(total)[:, :, None]).reshape(q_count, width)


def body(
    tokens,
    pair,
    token_chain_index,
    key_mask,
    norm_gain,
    pair_gain,
    pair_proj,
    chain_gain,
    w_qkvg,
    w_out,
):
    width = tokens.shape[2]
    q_count = tokens.shape[1]
    k_count = pair.shape[1]
    heads = chain_gain.shape[0]
    normalized_input = norm_rows(tokens, norm_gain).astype(jnp.bfloat16)
    query_weight = w_qkvg[:, :width]
    w_pairs = w_qkvg[:, width : 3 * width]
    gate_weight = w_qkvg[:, 3 * width :]
    query_vectors = jnp.einsum(
        "fop,pu->fou", normalized_input, query_weight, preferred_element_type=jnp.float32
    ).astype(jnp.bfloat16)
    gate_values = jnp.einsum(
        "fop,pu->fou", normalized_input, gate_weight, preferred_element_type=jnp.float32
    ).astype(jnp.bfloat16)
    row_start = lax.axis_index("pb") * q_count
    col_start = lax.axis_index("ka") * k_count
    chain_query = lax.dynamic_slice_in_dim(token_chain_index, row_start, q_count)
    chain_keys = lax.dynamic_slice_in_dim(token_chain_index, col_start, k_count)
    bias = pair_bias(pair, pair_gain, pair_proj, chain_query, chain_keys, chain_gain)
    key_values = jnp.einsum(
        "fop,pu->fou",
        lax.all_gather(normalized_input, "pb", axis=1, tiled=True),
        w_pairs,
        preferred_element_type=jnp.float32,
    ).astype(jnp.bfloat16)
    bias_all = lax.all_gather(bias, "ka", axis=2, tiled=True)

    def one_sample(items):
        query_one, pairs_one = items
        return apply_attention(
            query_one, pairs_one[:, :width], pairs_one[:, width:], bias_all, key_mask, heads
        )

    attended = lax.map(one_sample, (query_vectors, key_values))
    hidden = (jax.nn.sigmoid(gate_values.astype(jnp.float32)) * attended).astype(jnp.bfloat16)
    return jnp.einsum("sqd,de->sqe", hidden, w_out, preferred_element_type=jnp.float32).astype(
        jnp.bfloat16
    )


def solution(mesh):
    in_specs = (P("ka", "pb", None), P("pb", "ka", None), P(), P(), P(), P(), P(), P(), P(), P())
    out_specs = P("ka", "pb", None)
    return jax.shard_map(body, mesh=mesh, in_specs=in_specs, out_specs=out_specs, check_vma=False)
```

profile of v0, /device:TPU:1, one launch (start us, length us, event | category | flops | bytes accessed | tf_op | source)
XLA Modules:
  0.0 251.6 jit_solution(10574960976641568531)
XLA Ops:
  6.5 0.0 copy-start
  6.5 0.0 all-gather.3.cloned.1.call-start
  6.5 1.1 convert_reduce_fusion.1
  7.7 1.1 fusion.60
  8.8 0.0 copy-start.5
  8.8 0.0 copy-start.6
  8.8 1.8 fusion.62
  10.6 0.0 all-gather.3.cloned.1.call-update
  10.7 0.0 all-gather.5.cloned.1.call-start
  10.7 0.0 copy-start.1
  10.7 0.9 fusion.70
  11.7 0.1 compare_convert_fusion
  11.7 3.6 %convert_reduce_fusion = f32[128,128]{1,0:T(8,128)S(1)} fusion(bf16[128,128,128]{2,1,0:T(8,128)(2,1)} %param.11), kind=kLoop, calls=%fused_computation.5 | loop fusion | flops 4177920 | bytes 4259840 | tf_op jit(solution)/shard_map/reduce_sum | solution.py:11
  15.4 0.0 copy-done.1
  15.4 4.8 %fusion.4 = f32[128,128]{1,0:T(8,128)S(1)} fusion(bf16[128,128,128]{2,1,0:T(8,128)(2,1)S(1)} %copy-done.1, f32[128,128]{1,0:T(8,128)S(1)} %broadcast_multiply_fusion), kind=kLoop, calls=%fused_computation.8 | loop fusion | flops 8372224 | bytes 4325376 | tf_op jit(solution)/shard_map/reduce_sum | solution.py:12
  20.2 0.0 copy-start.4
  20.2 0.0 copy-done.5
  20.2 0.0 copy-done.6
  20.2 0.0 copy-start.2
  20.2 9.9 %fusion.6 = f32[128,128,16]{1,2,0:T(8,128)S(1)} fusion(bf16[128,128,128]{2,1,0:T(8,128)(2,1)S(1)} %copy-done.1, f32[128]{0:T(128)S(1)} %copy-done.6, f32[128,128]{1,0:T(8,128)S(1)} %add_rsqrt_fusion, f32[128,128]{1,0:T(8,128)S(1)} %broadcast_multiply_fusion, f32[128,16]{0,1:T(8,128)S(1)} %copy-done.5), kind=kOutput, calls=%fused_computation.10 | convolution fusion | flops 411041792 | bytes 5382656 | tf_op jit(solution)/shard_map/qkc,ch->hqk/dot_general | solution.py:18
  30.2 0.0 copy-done.4
  30.2 0.0 copy-start.3
  30.2 1.3 bitcast_add_fusion
  31.5 0.0 all-gather.5.cloned.1.call-update
  31.5 0.0 copy-done.2
  31.5 1.6 fusion.47
  33.2 0.2 copy.13
  33.3 0.0 copy-done.3
  33.3 71.1 %all-gather.3.cloned.1.call-done = bf16[1,2048,768]{2,1,0:T(8,128)(2,1)} async-done(((bf16[1,128,768]{2,1,0:T(8,128)(2,1)}), bf16[1,2048,768]{2,1,0:T(8,128)(2,1)}) %all-gather.3.cloned.1.call-update) | async-done | bytes 3145744 | tf_op jit(solution)/shard_map/all_gather | solution.py:76
  104.4 7.5 %convolution_convert_fusion = bf16[2048,1536]{0,1:T(8,128)(2,1)S(1)} fusion(bf16[1,2048,768]{2,1,0:T(8,128)(2,1)} %all-gather.3.cloned.1.call-done, bf16[768,3072]{1,0:T(8,128)(2,1)} %param.18), kind=kOutput, calls=%fused_computation.13 | convolution fusion | flops 4834983936 | bytes 11796480 | tf_op jit(solution)/shard_map/fop,pu->fou/dot_general | solution.py:74
  111.9 3.2 %fusion.69 = (bf16[2048,768]{0,1:T(8,128)(2,1)}, bf16[2048,768]{0,1:T(8,128)(2,1)}) fusion(bf16[2048,1536]{0,1:T(8,128)(2,1)S(1)} %convolution_convert_fusion), kind=kLoop, calls=%fused_computation.55 | loop fusion | bytes 12582912 | tf_op jit(solution)/shard_map/while/body/eval_jaxpr/slice | solution.py:85
  115.1 93.2 %all-gather.5.cloned.1.call-done = f32[16,128,2048]{2,1,0:T(8,128)} async-done(((f32[16,128,128]{2,1,0:T(8,128)}), f32[16,128,2048]{2,1,0:T(8,128)}) %all-gather.5.cloned.1.call-update) | async-done | bytes 16777232 | tf_op jit(solution)/shard_map/all_gather | solution.py:80
  208.3 15.5 %fusion.71 = (f32[16,128]{1,0:T(8,128)S(1)}, f32[16,128,2048]{2,1,0:T(8,128)}) fusion(f32[16,128,2048]{2,1,0:T(8,128)} %all-gather.5.cloned.1.call-done, bf16[128,16,48]{0,2,1:T(8,128)(2,1)S(1)} %bitcast.31, bf16[2048,16,48]{0,2,1:T(8,128)(2,1)} %bitcast.30, pred[2048]{0:T(1024)(128)(4,1)S(1)} %broadcast_compare_fusion), kind=kOutput, calls=%fused_computation.57 | convolution fusion | flops 419428352 | bytes 36907008 | tf_op jit(solution)/shard_map/while/body/eval_jaxpr/qhd,khd->hqk/dot_general | solution.py:31
  223.8 8.1 %fusion = f32[16,128]{1,0:T(8,128)S(1)} fusion(f32[16,128,2048]{2,1,0:T(8,128)} %get-tuple-element.28, f32[16,128]{1,0:T(8,128)S(1)} %get-tuple-element.26), kind=kLoop, calls=%fused_computation.2 | loop fusion | flops 8386560 | bytes 16793600 | tf_op jit(solution)/shard_map/while/body/eval_jaxpr/reduce_sum | solution.py:36
  231.9 9.8 %fusion.55 = f32[128,16,48]{0,2,1:T(8,128)S(1)} fusion(bf16[2048,16,48]{0,2,1:T(8,128)(2,1)} %bitcast.29, f32[16,128,2048]{2,1,0:T(8,128)} %get-tuple-element.28, f32[16,128]{1,0:T(8,128)S(1)} %get-tuple-element.26, f32[128,16]{0,1:T(8,128)S(1)} %bitcast.33), kind=kOutput, calls=%fused_computation.36 | convolution fusion | flops 411140096 | bytes 20332544 | tf_op jit(solution)/shard_map/while/body/eval_jaxpr/hqk,khd->qhd/dot_general | solution.py:37
  241.8 0.0 copy-done
  241.8 3.0 %fusion.52 = bf16[1,128,768]{2,1,0:T(8,128)(2,1)} fusion(bf16[768,768]{1,0:T(8,128)(2,1)S(1)} %copy-done, f32[128,768]{0,1:T(8,128)S(1)} %bitcast.32, bf16[768,3072]{1,0:T(8,128)(2,1)} %param.18, bf16[1,128,768]{2,1,0:T(8,128)(2,1)S(1)} %copy-done.2), kind=kOutput, calls=%fused_computation.34 | convolution fusion | flops 302776320 | bytes 3145728 | tf_op jit(solution)/shard_map/sqd,de->sqe/dot_general | solution.py:90
  (5 shorter events, 0.0 us)
Async XLA Ops:
  6.5 235.3 %copy-start = (bf16[768,768]{1,0:T(8,128)(2,1)S(1)}, bf16[768,768]{1,0:T(8,128)(2,1)}, u32[]{:S(2)}) copy-start(bf16[768,768]{1,0:T(8,128)(2,1)} %param.19) | copy-start | bytes 3538948
  6.5 97.9 %all-gather.3.cloned.1.call-start = ((), (), s32[]{:S(2)}) async-start(), calls=%async_computation | async-start | bytes 3342336 | tf_op jit(solution)/shard_map/all_gather | solution.py:76
  8.8 11.4 %copy-start.5 = (f32[128,16]{0,1:T(8,128)S(1)}, f32[128,16]{0,1:T(8,128)}, u32[]{:S(2)}) copy-start(f32[128,16]{0,1:T(8,128)} %param.16) | copy-start | bytes 24580
  8.8 11.4 %copy-start.6 = (f32[128]{0:T(128)S(1)}, f32[128]{0:T(128)}, u32[]{:S(2)}) copy-start(f32[128]{0:T(128)} %param.15) | copy-start | bytes 1540
  10.7 197.7 %all-gather.5.cloned.1.call-start = ((), (), s32[]{:S(2)}) async-start(), calls=%async_computation.1 | async-start | bytes 17825792 | tf_op jit(solution)/shard_map/all_gather | solution.py:80
  10.7 4.7 %copy-start.1 = (bf16[128,128,128]{2,1,0:T(8,128)(2,1)S(1)}, bf16[128,128,128]{2,1,0:T(8,128)(2,1)}, u32[]{:S(2)}) copy-start(bf16[128,128,128]{2,1,0:T(8,128)(2,1)} %param.11) | copy-start | bytes 12582916
  20.2 10.0 %copy-start.4 = (f32[16]{0:T(128)S(1)}, f32[16]{0:T(128)}, u32[]{:S(2)}) copy-start(f32[16]{0:T(128)} %param.17) | copy-start | bytes 196
  20.2 11.3 %copy-start.2 = (bf16[1,128,768]{2,1,0:T(8,128)(2,1)S(1)}, bf16[1,128,768]{2,1,0:T(8,128)(2,1)}, u32[]{:S(2)}) copy-start(bf16[1,128,768]{2,1,0:T(8,128)(2,1)} %fusion.62) | copy-start | bytes 589828
  30.2 3.2 %copy-start.3 = (s32[2048]{0:T(1024)S(1)}, s32[2048]{0:T(1024)}, u32[]{:S(2)}) copy-start(s32[2048]{0:T(1024)} %param.13) | copy-start | bytes 24580
Sparse Core Ops, SparseCore 0:
  10.8 93.5 all-gather.2
  106.2 102.1 all-gather.4
where the time goes:
time: 252 us
  waiting for transfers between devices  164 us (65%)
  matrix products  47.3 us (19%)
  other arithmetic  22 us (9%)
  between operations  13.6 us (5%)
  local copies, waits for them, and re-layouts  4.3 us (2%)
    all_gather x1, waiting for transfers between devices, body(): bias_all = lax.all_gather(bias, 'ka', axis=2, tiled=True)  93.2 us
    all_gather x1, waiting for transfers between devices, body(): lax.all_gather(normalized_input, 'pb', axis=1, tiled=True)  71.1 us
    dot_general x1, matrix products, apply_attention(): jnp.einsum('qhd,khd->hqk', query_heads, key_heads, preferred_element_type...  15.5 us
    dot_general x1, matrix products, pair_bias(): jnp.einsum('qkc,ch->hqk', zhat, pair_proj, precision=lax.Precision.HIGHEST)  9.91 us
    dot_general x1, matrix products, apply_attention(): jnp.einsum('hqk,khd->qhd', expo.astype(jnp.bfloat16), value_heads, prefer...  9.84 us
    reduce_sum x1, other arithmetic, apply_attention(): total = jnp.sum(expo, axis=-1)  8.14 us
    dot_general x1, matrix products, body(): jnp.einsum('fop,pu->fou', lax.all_gather(normalized_input, 'pb', axis=1,...  7.49 us
    reduce_sum x2, other arithmetic, norm_rows(): spread = jnp.mean(jnp.square(values - center), axis=-1, keepdims=True)  5.9 us
  transfers between devices with their start and end apart: 2, of which 2 were waited for; matrix products, arithmetic and copies ran while one was open for 13% of the time, Pallas kernels for 0%

commit v1 on v0

--- a/solution.py
+++ b/solution.py
@@ -77,7 +77,9 @@
         w_pairs,
         preferred_element_type=jnp.float32,
     ).astype(jnp.bfloat16)
-    bias_all = lax.all_gather(bias, "ka", axis=2, tiled=True)
+    bias_all = jnp.concatenate(
+        lax.all_to_all(jnp.stack([bias] * lax.axis_size("ka")), "ka", 0, 0), axis=2
+    )
 
     def one_sample(items):
         query_one, pairs_one = items

time: 252 us -> 356 us (1.41)
  waiting for transfers between devices: 164 us -> 257 us
  starting transfers between devices: 0.04 us -> 8.47 us
  local copies, waits for them, and re-layouts: 4.3 us -> 12.6 us
  other arithmetic: 22 us -> 17.7 us
    all_gather x1, waiting for transfers between devices: 71.1 us -> 185 us  [body(): lax.all_gather(normalized_input, 'pb', axis=1, tiled=True)]
    all_gather x1 -> x0, waiting for transfers between devices: 93.2 us -> none  [body(): bias_all = lax.all_gather(bias, 'ka', axis=2, tiled=True)]
    all_to_all x0 -> x1, waiting for transfers between devices: none -> 72.4 us  [body(): lax.all_to_all(jnp.stack([bias] * lax.axis_size('ka')), 'ka', 0, 0)]
    all_to_all x0 -> x1, starting transfers between devices: none -> 8.25 us  [body(): lax.all_to_all(jnp.stack([bias] * lax.axis_size('ka')), 'ka', 0, 0)]
    another operation x0 -> x1, local copies, waits for them, and re-layouts: none -> 7.83 us  [body(): jnp.stack([bias] * lax.axis_size('ka'))]
  transfers between devices with their start and end apart: 2 -> 2, of which waited for: 2 -> 2; matrix products, arithmetic and copies ran while one was open for 13% -> 4% of each run, Pallas kernels for 0% -> 0%
where the time goes in v1:
time: 356 us; the launch traced here: 355 us
  waiting for transfers between devices  257 us (72%)
  matrix products  46 us (13%)
  other arithmetic  17.7 us (5%)
  between operations  13.6 us (4%)
  local copies, waits for them, and re-layouts  12.6 us (4%)
  starting transfers between devices  8.47 us (2%)
    all_gather x1, waiting for transfers between devices, body(): lax.all_gather(normalized_input, 'pb', axis=1, tiled=True)  185 us
    all_to_all x1, waiting for transfers between devices, body(): lax.all_to_all(jnp.stack([bias] * lax.axis_size('ka')), 'ka', 0, 0)  72.4 us
    dot_general x1, matrix products, pair_bias(): jnp.einsum('qkc,ch->hqk', zhat, pair_proj, precision=lax.Precision.HIGHEST)  12.3 us
    dot_general x1, matrix products, apply_attention(): jnp.einsum('qhd,khd->hqk', query_heads, key_heads, preferred_element_type...  12 us
    dot_general x1, matrix products, apply_attention(): jnp.einsum('hqk,khd->qhd', expo.astype(jnp.bfloat16), value_heads, prefer...  9.87 us
    all_to_all x1, starting transfers between devices, body(): lax.all_to_all(jnp.stack([bias] * lax.axis_size('ka')), 'ka', 0, 0)  8.25 us
    reduce_sum x1, other arithmetic, apply_attention(): total = jnp.sum(expo, axis=-1)  8.14 us
    another operation x1, local copies, waits for them, and re-layouts, body(): jnp.stack([bias] * lax.axis_size('ka'))  7.83 us
  transfers between devices with their start and end apart: 2, of which 2 were waited for; matrix products, arithmetic and copies ran while one was open for 4% of the time, Pallas kernels for 0%

profile of v1, /device:TPU:1, one launch (start us, length us, event | category | flops | bytes accessed | tf_op | source)
XLA Modules:
  0.0 355.5 jit_solution(1330198322428591047)
XLA Ops:
  6.5 0.0 copy-start
  6.5 0.0 copy-start.8
  6.5 0.0 copy-start.6
  6.5 0.0 copy-start.7
  6.5 0.0 copy-start.1
  6.6 3.5 convert_reduce_fusion
  10.1 0.0 copy-done.1
  10.1 4.8 %fusion.5 = f32[128,128]{1,0:T(8,128)S(1)} fusion(bf16[128,128,128]{2,1,0:T(8,128)(2,1)S(1)} %copy-done.1, f32[128,128]{1,0:T(8,128)S(1)} %broadcast_multiply_fusion), kind=kLoop, calls=%fused_computation.9 | loop fusion | flops 8372224 | bytes 4325376 | tf_op jit(solution)/shard_map/reduce_sum | solution.py:12
  14.9 0.8 fusion.77
  15.7 0.1 compare_convert_fusion
  15.8 0.0 copy-done.8
  15.8 0.0 copy-done.6
  15.9 0.0 copy-done.7
  15.9 12.3 %fusion.20 = f32[16,128,128]{2,0,1:T(8,128)S(1)} fusion(bf16[128,128,128]{2,1,0:T(8,128)(2,1)} %param.11, f32[128]{0:T(128)S(1)} %copy-done.7, f32[128,128]{1,0:T(8,128)S(1)} %add_rsqrt_fusion, f32[128,128]{1,0:T(8,128)S(1)} %broadcast_multiply_fusion, f32[128,128]{1,0:T(8,128)S(1)} %compare_convert_fusion, f32[16]{0:T(128)S(1)} %copy-done.8, ...), kind=kOutput, calls=%fused_computation.21 | convolution fusion | flops 411566080 | bytes 5448256 | tf_op jit(solution)/shard_map/qkc,ch->hqk/dot_general | solution.py:18
  28.2 0.3 copy.20
  28.5 7.8 %stack.2 = f32[16,16,128,128]{3,2,1,0:T(8,128)} broadcast(f32[16,128,128]{2,1,0:T(8,128)S(1)} %copy.20), dimensions={1,2,3} | broadcast | bytes 17825792 | tf_op jit(solution)/shard_map/stack | solution.py:81
  36.4 0.0 copy-start.2
  36.4 0.0 copy-start.5
  36.4 0.0 copy-start.4
  36.4 8.3 %all-to-all-start = ((f32[16,16,128,128]{3,2,1,0:T(8,128)}), f32[16,16,128,128]{3,2,1,0:T(8,128)}, u32[]{:S(2)}, u32[]{:S(2)}) async-start(f32[16,16,128,128]{3,2,1,0:T(8,128)} %stack.2), calls=%async_computation | async-start | bytes 33554432 | tf_op jit(solution)/shard_map/all_to_all | solution.py:81
  44.6 0.2 all-gather.2.cloned.1.call-start
  44.9 0.0 copy-done.2
  44.9 0.1 convert_reduce_fusion.1
  45.0 0.2 fusion.67
  45.2 0.0 copy-done.5
  45.2 0.8 fusion.69
  46.1 0.0 all-gather.2.cloned.1.call-update
  46.1 1.7 fusion.54
  47.8 0.2 copy.19
  48.0 0.0 copy-done.4
  48.0 184.7 %all-gather.2.cloned.1.call-done = bf16[1,2048,768]{2,1,0:T(8,128)(2,1)} async-done(((bf16[1,128,768]{2,1,0:T(8,128)(2,1)}), bf16[1,2048,768]{2,1,0:T(8,128)(2,1)}) %all-gather.2.cloned.1.call-update) | async-done | bytes 3145744 | tf_op jit(solution)/shard_map/all_gather | solution.py:76
  232.7 7.5 %convolution_convert_fusion = bf16[2048,1536]{0,1:T(8,128)(2,1)S(1)} fusion(bf16[1,2048,768]{2,1,0:T(8,128)(2,1)} %all-gather.2.cloned.1.call-done, bf16[768,3072]{1,0:T(8,128)(2,1)} %param.18), kind=kOutput, calls=%fused_computation.14 | convolution fusion | flops 4834983936 | bytes 11796480 | tf_op jit(solution)/shard_map/fop,pu->fou/dot_general | solution.py:74
  240.2 3.2 fusion.76
  243.4 72.4 %all-to-all-done = f32[16,16,128,128]{3,2,1,0:T(8,128)} async-done(((f32[16,16,128,128]{3,2,1,0:T(8,128)}), f32[16,16,128,128]{3,2,1,0:T(8,128)}, u32[]{:S(2)}, u32[]{:S(2)}) %all-to-all-start) | async-done | bytes 16777248 | tf_op jit(solution)/shard_map/all_to_all | solution.py:81
  315.8 12.0 %fusion.78 = (f32[16,128]{1,0:T(8,128)S(1)}, f32[16,128,2048]{2,1,0:T(8,128)}) fusion(bf16[128,16,48]{0,2,1:T(8,128)(2,1)S(1)} %bitcast.42, bf16[2048,16,48]{0,2,1:T(8,128)(2,1)} %bitcast.40, pred[2048]{0:T(1024)(128)(4,1)S(1)} %broadcast_compare_fusion, f32[16,16,128,128]{3,2,1,0:T(8,128)} %all-to-all-done), kind=kOutput, calls=%fused_computation.59 | convolution fusion | flops 419428352 | bytes 36907008 | tf_op jit(solution)/shard_map/while/body/eval_jaxpr/qhd,khd->hqk/dot_general | solution.py:31
  327.8 8.1 %fusion.1 = f32[16,128]{1,0:T(8,128)S(1)} fusion(f32[16,128,2048]{2,1,0:T(8,128)} %get-tuple-element.28, f32[16,128]{1,0:T(8,128)S(1)} %get-tuple-element.26), kind=kLoop, calls=%fused_computation.3 | loop fusion | flops 8386560 | bytes 16793600 | tf_op jit(solution)/shard_map/while/body/eval_jaxpr/reduce_sum | solution.py:36
  336.0 0.0 copy-start.3
  336.0 9.9 %fusion.62 = f32[128,16,48]{0,2,1:T(8,128)S(1)} fusion(bf16[2048,16,48]{0,2,1:T(8,128)(2,1)} %bitcast.39, f32[16,128,2048]{2,1,0:T(8,128)} %get-tuple-element.28, f32[16,128]{1,0:T(8,128)S(1)} %get-tuple-element.26, f32[128,16]{0,1:T(8,128)S(1)} %bitcast.43), kind=kOutput, calls=%fused_computation.38 | convolution fusion | flops 411140096 | bytes 20332544 | tf_op jit(solution)/shard_map/while/body/eval_jaxpr/hqk,khd->qhd/dot_general | solution.py:37
  345.8 0.2 copy.22
  346.0 0.0 copy-done
  346.0 0.0 copy-done.3
  346.0 2.6 fusion.59
  (5 shorter events, 0.0 us)
Async XLA Ops:
  6.5 339.5 %copy-start = (bf16[768,768]{1,0:T(8,128)(2,1)S(1)}, bf16[768,768]{1,0:T(8,128)(2,1)}, u32[]{:S(2)}) copy-start(bf16[768,768]{1,0:T(8,128)(2,1)} %param.19) | copy-start | bytes 3538948
  6.5 9.3 %copy-start.8 = (f32[16]{0:T(128)S(1)}, f32[16]{0:T(128)}, u32[]{:S(2)}) copy-start(f32[16]{0:T(128)} %param.17) | copy-start | bytes 196
  6.5 9.3 %copy-start.6 = (f32[128,16]{0,1:T(8,128)S(1)}, f32[128,16]{0,1:T(8,128)}, u32[]{:S(2)}) copy-start(f32[128,16]{0,1:T(8,128)} %param.16) | copy-start | bytes 24580
  6.5 9.3 %copy-start.7 = (f32[128]{0:T(128)S(1)}, f32[128]{0:T(128)}, u32[]{:S(2)}) copy-start(f32[128]{0:T(128)} %param.15) | copy-start | bytes 1540
  6.5 3.5 copy-start.1
  36.4 8.5 %copy-start.2 = (bf16[1,128,768]{2,1,0:T(8,128)(2,1)S(1)}, bf16[1,128,768]{2,1,0:T(8,128)(2,1)}, u32[]{:S(2)}) copy-start(bf16[1,128,768]{2,1,0:T(8,128)(2,1)} %param.10) | copy-start | bytes 589828
  36.4 8.8 %copy-start.5 = (f32[768]{0:T(1024)S(1)}, f32[768]{0:T(1024)}, u32[]{:S(2)}) copy-start(f32[768]{0:T(1024)} %param.14) | copy-start | bytes 9220
  36.4 11.6 %copy-start.4 = (s32[2048]{0:T(1024)S(1)}, s32[2048]{0:T(1024)}, u32[]{:S(2)}) copy-start(s32[2048]{0:T(1024)} %param.13) | copy-start | bytes 24580
  36.4 279.4 %all-to-all-start = ((f32[16,16,128,128]{3,2,1,0:T(8,128)}), f32[16,16,128,128]{3,2,1,0:T(8,128)}, u32[]{:S(2)}, u32[]{:S(2)}) async-start(f32[16,16,128,128]{3,2,1,0:T(8,128)} %stack.2), calls=%async_computation | async-start | bytes 33554432 | tf_op jit(solution)/shard_map/all_to_all | solution.py:81
  44.6 188.1 %all-gather.2.cloned.1.call-start = ((), (), s32[]{:S(2)}) async-start(), calls=%async_computation.1 | async-start | bytes 3342336 | tf_op jit(solution)/shard_map/all_gather | solution.py:76
  336.0 10.1 %copy-start.3 = (bf16[1,128,768]{2,1,0:T(8,128)(2,1)S(1)}, bf16[1,128,768]{2,1,0:T(8,128)(2,1)}, u32[]{:S(2)}) copy-start(bf16[1,128,768]{2,1,0:T(8,128)(2,1)} %fusion.69) | copy-start | bytes 589828
Sparse Core Ops, SparseCore 0:
  48.1 184.6 all-gather.1
